TPU v7x, 32 devices: a whole 2x2x4 slice. The times are simulated.
32 devices in a mesh: grp: 2 (over x), wide: 8 (over z, y), narrow: 2 (over core).
Axes of the slice: x: 2, y: 2, z: 4, core: 2. Of those that a mesh axis runs over, the one named last changes fastest.
Arguments:
- video: bfloat16 [16, 64, 32, 128], P(('grp', 'wide')), parts along dimension 0, may hold values from -6 to 6
- spatial_weight: bfloat16 [144, 9, 64], replicated, may hold values from -0.25 to 0.25
- spatial_bias: float32 [144], replicated, may hold values from -4 to 4
- temporal_weight: bfloat16 [64, 9, 144], replicated, may hold values from -0.15625 to 0.15625
- temporal_bias: float32 [64], replicated, may hold values from -4 to 4
- out_cotangent: bfloat16 [8, 64, 32, 128], P('grp', None, ('wide', 'narrow')), parts along dimension 0, may hold values from -6 to 6
Outputs:
- output: bfloat16 [8, 64, 32, 128], P('grp', None, ('wide', 'narrow')), parts along dimension 0
- grad_video: bfloat16 [16, 64, 32, 128], P(('grp', 'wide'), None, 'narrow'), parts along dimension 0
- grad_spatial: float32 [288, 9, 64], P(('grp', 'narrow')), parts along dimension 0
- grad_temporal: float32 [128, 9, 144], P('grp'), parts along dimension 0
There are 2 independent parts, one for each index of `grp`. A program takes and returns all parts, laid end to end along the dimension named above; an argument that names none is the same for every part. Nothing has to cross between parts.
All inputs are finite; a program needn't handle non-finite values.
Results may differ from a plain program's by a relative error of at most 0.0058.
Values may be sent and summed in bfloat16 or wider, within the bound.
A program may use at most 128 MiB of HBM per device.

v0:
```python
import math

import jax
import jax.numpy as jnp
from jax import lax
from jax.sharding import PartitionSpec as P


def silu_slope(preact):
    logistic = jax.nn.sigmoid(preact)
    return logistic * (1.0 + preact * (1.0 - logistic))


def shifted_slabs(padded, row_count, col_count, reverse_taps):
    slab_list = []
    for row_shift in range(3):
        start_row = 2 - row_shift if reverse_taps else row_shift
        pieces = []
        for col_shift in range(3):
            start_col = 2 - col_shift if reverse_taps else col_shift
            pieces.append(
                padded[:, :, start_row : start_row + row_count, start_col : start_col + col_count]
            )
        slab_list.append(jnp.stack(pieces, axis=1))
    return slab_list


def grad_input(padded_grad, weights_grid, row_count, col_count):
    slab_list = shifted_slabs(padded_grad, row_count, col_count, True)
    result = None
    for row_shift in range(3):
        contribution = jnp.einsum(
            "ojc,fjoyx->fcyx",
            weights_grid[:, row_shift],
            slab_list[row_shift],
            preferred_element_type=jnp.float32,
        )
        result = contribution if result is None else result + contribution
    return result


def spatial_forward(slab_list, weights_grid, bias):
    result = bias[None, :, None, None]
    for row_shift in range(3):
        result = result + jnp.einsum(
            "ojc,fjcyx->foyx",
            weights_grid[:, row_shift],
            slab_list[row_shift],
            preferred_element_type=jnp.float32,
        )
    return result


def kernel_terms(grad_pre, slab_list):
    stacked = jnp.stack(
        [
            jnp.einsum(
                "foyx,fjcyx->ojc",
                grad_pre,
                slab_list[row_shift],
                preferred_element_type=jnp.float32,
            )
            for row_shift in range(3)
        ],
        axis=1,
    )
    return stacked.reshape(stacked.shape[0], 9, stacked.shape[3])


def frame_stack(frames, tap_count, out_count):
    half_taps = tap_count // 2
    padded = jnp.pad(frames, ((half_taps, half_taps), (0, 0), (0, 0)))
    paired = padded.reshape((padded.shape[0] // 2, 2) + frames.shape[1:])
    return jnp.stack(
        [paired[offset // 2 : offset // 2 + out_count, offset % 2] for offset in range(tap_count)],
        axis=1,
    )


def per_device(video, spatial_weight, spatial_bias, temporal_weight, temporal_bias, out_cotangent):
    wide_count = lax.axis_size("wide")
    core_count = lax.axis_size("narrow")
    core_index = lax.axis_index("narrow")
    frame_local, in_chan, row_count, col_count = video.shape
    chan_full = spatial_weight.shape[0]
    chan_local = chan_full // core_count
    tap_count = temporal_weight.shape[1]
    out_chan = temporal_weight.shape[0]
    out_count = out_cotangent.shape[0]
    tile_rows = out_cotangent.shape[2]
    tile_width = tile_rows * col_count
    frame_count = frame_local * wide_count
    half_taps = tap_count // 2
    full_grid = spatial_weight.reshape(chan_full, 3, 3, in_chan)
    cotangent_flat = out_cotangent.reshape(out_count, out_chan, tile_width)
    temporal_scale = 1.0 / math.sqrt(out_count * row_count * col_count)
    spatial_scale = 1.0 / math.sqrt(frame_count * row_count * col_count)
    weights_grid = lax.dynamic_slice_in_dim(full_grid, core_index * chan_local, chan_local, 0)
    own_bias = lax.dynamic_slice_in_dim(spatial_bias, core_index * chan_local, chan_local, 0)
    padded_video = jnp.pad(video, ((0, 0), (0, 0), (1, 1), (1, 1)))
    video_slabs = shifted_slabs(padded_video, row_count, col_count, False)
    preact = spatial_forward(video_slabs, weights_grid, own_bias)
    activation = jax.nn.silu(preact).astype(jnp.bfloat16)
    sectioned = activation.reshape(frame_local, chan_local, wide_count, core_count, tile_width)
    joined = lax.all_to_all(
        lax.all_to_all(sectioned, "wide", split_axis=2, concat_axis=0, tiled=True),
        "narrow",
        split_axis=3,
        concat_axis=1,
        tiled=True,
    )
    tile = joined.reshape(joined.shape[0], joined.shape[1], joined.shape[4])
    patches = frame_stack(tile, tap_count, out_count)
    combined = jnp.einsum(
        "okc,tkcq->toq", temporal_weight, patches, preferred_element_type=jnp.float32
    )
    combined = combined + temporal_bias[None, :, None]
    combined, patches = (combined[:, :, None, :], patches)
    output = combined.astype(jnp.bfloat16).reshape(out_count, out_chan, tile_rows, col_count)
    local_temporal = jnp.einsum(
        "toq,tkcq->okc", cotangent_flat, patches, preferred_element_type=jnp.float32
    )
    spaced = jnp.stack([cotangent_flat, jnp.zeros_like(cotangent_flat)], axis=1).reshape(
        2 * out_count, out_chan, tile_width
    )
    spaced = jnp.pad(spaced, ((half_taps, half_taps), (0, 0), (0, 0)))
    cot_patches = jnp.stack(
        [
            spaced[tap_count - 1 - offset : tap_count - 1 - offset + frame_count]
            for offset in range(tap_count)
        ],
        axis=1,
    )
    grad_tile = jnp.einsum(
        "okc,fkoq->fcq", temporal_weight, cot_patches, preferred_element_type=jnp.float32
    )
    local_temporal, grad_tile = (local_temporal, grad_tile.astype(jnp.bfloat16))
    grad_temporal = lax.psum(local_temporal * temporal_scale, ("wide", "narrow"))
    shaped = grad_tile.reshape(frame_count, chan_full, 1, 1, tile_width)
    split_cores = lax.all_to_all(shaped, "narrow", split_axis=1, concat_axis=3, tiled=True)
    returned = lax.all_to_all(split_cores, "wide", split_axis=0, concat_axis=2, tiled=True)
    grad_act = returned.reshape(frame_local, chan_local, row_count, col_count)
    grad_pre = (grad_act.astype(jnp.float32) * silu_slope(preact)).astype(jnp.bfloat16)
    local_spatial = kernel_terms(grad_pre, video_slabs)
    grad_spatial = lax.psum(local_spatial * spatial_scale, "wide")
    padded_grad = jnp.pad(grad_pre, ((0, 0), (0, 0), (1, 1), (1, 1)))
    partial_image = grad_input(padded_grad, weights_grid, row_count, col_count)
    grad_video = lax.psum_scatter(partial_image, "narrow", scatter_dimension=2, tiled=True).astype(
        jnp.bfloat16
    )
    return (output, grad_video, grad_spatial, grad_temporal)


def solution(mesh):
    in_specs = (
        P(("grp", "wide"), None, None, None),
        P(),
        P(),
        P(),
        P(),
        P("grp", None, ("wide", "narrow"), None),
    )
    out_specs = (
        P("grp", None, ("wide", "narrow"), None),
        P(("grp", "wide"), None, "narrow", None),
        P(("grp", "narrow"), None, None),
        P("grp", None, None),
    )
    return jax.shard_map(
        per_device, mesh=mesh, in_specs=in_specs, out_specs=out_specs, check_vma=False
    )
```

profile of v0, /device:TPU:0, one launch (start us, length us, event | category | flops | bytes accessed | tf_op | source)
XLA Modules:
  0.0 237.4 jit_solution(4449729186291158339)
XLA Ops:
  8.0 1.0 stack_reshape.3
  9.3 0.8 copy-done.1
  10.1 0.7 fusion.26
  11.0 4.3 %all_to_all.60 = bf16[8,144,1,1,256]{4,0,3,2,1:T(8,128)(2,1)S(1)} all-to-all(bf16[8,144,1,1,256]{4,0,3,2,1:T(8,128)(2,1)S(1)} %copy.89), channel_id=1, replica_groups=mesh['grp'=2,'wide'=8,'narrow'=2] {'narrow'}, dimensions={1} | all-to-all | bytes 1179648 | tf_op jit(solution)/shard_map/all_to_all | solution.py:140
  15.3 1.4 copy.111
  16.7 7.3 %all-to-all-start.3 = ((bf16[8,72,1,2,256]{4,3,1,2,0:T(2,128)(2,1)}), bf16[8,72,1,2,256]{4,3,1,2,0:T(2,128)(2,1)S(1)}, u32[]{:S(2)}, u32[]{:S(2)}) async-start(bf16[8,72,1,2,256]{4,3,1,2,0:T(2,128)(2,1)} %bitcast.280), calls=%async_computation.3 | async-start | bytes 1179648 | tf_op jit(solution)/shard_map/all_to_all | solution.py:141
  24.4 2.0 fusion.49
  27.9 1.6 fusion.16
  29.5 10.8 %all-to-all-done.3 = bf16[8,72,1,2,256]{4,3,1,2,0:T(2,128)(2,1)S(1)} async-done(((bf16[8,72,1,2,256]{4,3,1,2,0:T(2,128)(2,1)}), bf16[8,72,1,2,256]{4,3,1,2,0:T(2,128)(2,1)S(1)}, u32[]{:S(2)}, u32[]{:S(2)}) %all-to-all-start.3) | async-done | bytes 589856 | tf_op jit(solution)/shard_map/all_to_all | solution.py:141
  40.6 0.7 copy.91
  41.3 0.9 reshape.115
  42.3 3.0 %fusion.29 = (bf16[1,72,32,128]{3,1,2,0:T(8,128)(2,1)S(1)}, bf16[1,72,32,128]{3,1,2,0:T(8,128)(2,1)S(1)}) fusion(f32[1,72,32,128]{3,2,1,0:T(8,128)S(1)} %reshape.115, f32[1,32,128,72]{2,3,1,0:T(8,128)} %fusion.16, bf16[144,3,3,64]{0,3,2,1:T(8,128)(2,1)S(1)} %bitcast.282, s32[]{:T(128)S(6)} %select_n.4, s32[]{:T(128)S(6)} %add.85, ...), kind=kOutput, calls=%fused_computation.58 | convolution fusion | flops 118358016 | bytes 5160968 | tf_op jit(solution)/shard_map/ojc,fjcyx->foyx/dot_general | solution.py:45
  45.3 1.1 fusion.33
  46.4 0.6 fusion.20
  47.0 0.6 fusion.19
  47.6 1.6 fusion.24
  49.7 1.2 copy.78
  50.9 3.6 %all-to-all-start = ((bf16[1,72,8,2,256]{4,3,1,0,2:T(2,128)(2,1)}), bf16[1,72,8,2,256]{4,3,1,0,2:T(2,128)(2,1)S(1)}, u32[]{:S(2)}, u32[]{:S(2)}) async-start(bf16[1,72,8,2,256]{4,3,1,0,2:T(2,128)(2,1)} %copy.78), calls=%async_computation | async-start | bytes 1179648 | tf_op jit(solution)/shard_map/all_to_all | solution.py:106
  54.6 1.0 reshape.133
  55.6 1.7 convolution_bitcast_fusion.8
  59.3 0.8 maximum_multiply_fusion
  60.2 11.4 %all-to-all-done = bf16[1,72,8,2,256]{4,3,1,0,2:T(2,128)(2,1)S(1)} async-done(((bf16[1,72,8,2,256]{4,3,1,0,2:T(2,128)(2,1)}), bf16[1,72,8,2,256]{4,3,1,0,2:T(2,128)(2,1)S(1)}, u32[]{:S(2)}, u32[]{:S(2)}) %all-to-all-start) | async-done | bytes 589856 | tf_op jit(solution)/shard_map/all_to_all | solution.py:106
  71.8 4.2 %all_to_all.61 = bf16[8,72,1,2,256]{4,0,1,2,3:T(8,128)(2,1)S(1)} all-to-all(bf16[8,72,1,2,256]{4,0,1,2,3:T(8,128)(2,1)S(1)} %copy.79), channel_id=1, replica_groups=mesh['grp'=2,'wide'=8,'narrow'=2] {'narrow'}, dimensions={3} | all-to-all | bytes 1179648 | tf_op jit(solution)/shard_map/all_to_all | solution.py:105
  76.5 1.8 fusion.28
  78.4 0.6 fusion.32
  79.0 0.7 reshape.107
  79.7 1.1 convert_element_type.60
  80.8 0.9 copy.94
  81.7 50.6 %all-reduce.8.cloned.1.call-done = f32[72,9,64]{0,2,1:T(8,128)} async-done(((f32[72,9,64]{0,2,1:T(8,128)}), f32[72,9,64]{0,2,1:T(8,128)}) %all-reduce.8.cloned.1.call-update) | async-done | bytes 165904 | tf_op jit(solution)/shard_map/psum | solution.py:145
  132.3 94.1 %all-reduce.10.cloned.1.call-done = f32[64,9,144]{2,0,1:T(8,128)} async-done(((f32[64,9,144]{2,0,1:T(8,128)}), f32[64,9,144]{2,0,1:T(8,128)}) %all-reduce.10.cloned.1.call-update) | async-done | bytes 331792 | tf_op jit(solution)/shard_map/psum | solution.py:138
  226.4 1.7 copy.127
  228.1 1.9 copy.128
  (72 shorter events, 5.8 us)
Async XLA Ops:
  8.0 18.4 %copy-start = (bf16[144,9,64]{0,2,1:T(8,128)(2,1)S(1)}, bf16[144,9,64]{0,2,1:T(8,128)(2,1)}, u32[]{:S(2)}) copy-start(bf16[144,9,64]{0,2,1:T(8,128)(2,1)} %param.7) | copy-start | bytes 497668
  9.1 1.0 copy-start.1
  11.0 13.1 %copy-start.16 = (bf16[1,64,32,128]{3,2,1,0:T(8,128)(2,1)S(1)}, bf16[1,64,32,128]{3,2,1,0:T(8,128)(2,1)}, u32[]{:S(2)}) copy-start(bf16[1,64,32,128]{3,2,1,0:T(8,128)(2,1)} %param.6) | copy-start | bytes 1572868
  15.3 9.0 %copy-start.18 = (f32[144]{0:T(256)S(1)}, f32[144]{0:T(256)}, u32[]{:S(2)}) copy-start(f32[144]{0:T(256)} %param.8) | copy-start | bytes 1732
  16.7 23.5 %all-to-all-start.3 = ((bf16[8,72,1,2,256]{4,3,1,2,0:T(2,128)(2,1)}), bf16[8,72,1,2,256]{4,3,1,2,0:T(2,128)(2,1)S(1)}, u32[]{:S(2)}, u32[]{:S(2)}) async-start(bf16[8,72,1,2,256]{4,3,1,2,0:T(2,128)(2,1)} %bitcast.280), calls=%async_computation.3 | async-start | bytes 1179648 | tf_op jit(solution)/shard_map/all_to_all | solution.py:141
  24.0 55.7 %reduce-scatter.2.cloned.1.call-start = ((), (), s32[]{:S(2)}) async-start(), calls=%async_computation.5 | async-start | bytes 1572864 | tf_op jit(solution)/shard_map/reduce_scatter | solution.py:148
  26.4 0.8 copy-start.4
  26.4 1.0 copy-start.6
  26.4 1.2 copy-start.8
  26.4 1.3 copy-start.13
  26.4 1.5 copy-start.15
  45.3 1.1 copy-start.2
  49.3 6.3 %copy-start.3 = (bf16[1,72,32,128]{3,1,2,0:T(8,128)(2,1)S(1)}, bf16[1,72,32,128]{3,1,2,0:T(8,128)(2,1)}, u32[]{:S(2)}) copy-start(bf16[1,72,32,128]{3,1,2,0:T(8,128)(2,1)} %copy-done.2) | copy-start | bytes 1769476
  49.3 6.3 %copy-start.14 = (bf16[1,1,64,32,128]{4,2,3,1,0:T(8,128)(2,1)S(1)}, bf16[1,1,64,32,128]{4,2,3,1,0:T(8,128)(2,1)}, u32[]{:S(2)}) copy-start(bf16[1,1,64,32,128]{4,2,3,1,0:T(8,128)(2,1)} %copy-done.13) | copy-start | bytes 1572868
  50.9 20.7 %all-to-all-start = ((bf16[1,72,8,2,256]{4,3,1,0,2:T(2,128)(2,1)}), bf16[1,72,8,2,256]{4,3,1,0,2:T(2,128)(2,1)S(1)}, u32[]{:S(2)}, u32[]{:S(2)}) async-start(bf16[1,72,8,2,256]{4,3,1,0,2:T(2,128)(2,1)} %copy.78), calls=%async_computation | async-start | bytes 1179648 | tf_op jit(solution)/shard_map/all_to_all | solution.py:106
  54.5 77.7 %all-reduce.8.cloned.1.call-start = ((), (), s32[]{:S(2)}) async-start(), calls=%async_computation.6 | async-start | bytes 589824 | tf_op jit(solution)/shard_map/psum | solution.py:145
  55.6 1.8 copy-start.10
  55.6 1.8 copy-start.11
  55.6 1.8 copy-start.12
  57.4 1.0 copy-start.5
  57.4 1.2 copy-start.7
  57.4 1.3 copy-start.9
  60.1 166.3 %all-reduce.10.cloned.1.call-start = ((), (), s32[]{:S(2)}) async-start(), calls=%async_computation.7 | async-start | bytes 1179648 | tf_op jit(solution)/shard_map/psum | solution.py:138
  76.5 1.8 copy-start.17
Sparse Core Ops, SparseCore 0:
  49.3 7.5 reduce-scatter.1
Sparse Core Ops, SparseCore 1:
  60.2 72.0 all-reduce.7
  136.1 90.2 all-reduce.9
where the time goes:
time: 238 us; the launch traced here: 237 us
  waiting for transfers between devices  167 us (70%)
  local copies, waits for them, and re-layouts  18.9 us (8%)
  between operations  16 us (7%)
  matrix products  13.8 us (6%)
  starting transfers between devices  11 us (5%)
  blocking collectives  8.55 us (4%)
    psum x1, waiting for transfers between devices, per_device(): lax.psum(local_temporal * temporal_scale, ('wide', 'narrow'))  94.1 us
    psum x1, waiting for transfers between devices, per_device(): grad_spatial = lax.psum(local_spatial * spatial_scale, 'wide')  50.6 us
    all_to_all x1, waiting for transfers between devices, per_device(): lax.all_to_all(sectioned, 'wide', split_axis=2, concat_axis=0, tiled=True)  11.4 us
    all_to_all x1, waiting for transfers between devices, per_device(): lax.all_to_all(split_cores, 'wide', split_axis=0, concat_axis=2, tiled=True)  10.8 us
    unnamed x54, local copies, waits for them, and re-layouts  7.54 us
    all_to_all x1, starting transfers between devices, per_device(): lax.all_to_all(split_cores, 'wide', split_axis=0, concat_axis=2, tiled=True)  7.28 us
    dot_general x3, matrix products, spatial_forward(): jnp.einsum('ojc,fjcyx->foyx', weights_grid[:, row_shift], slab_list[row_s...  5.12 us
  transfers between devices with their start and end apart: 5, of which 4 were waited for; matrix products, arithmetic and copies ran while one was open for 7% of the time, Pallas kernels for 0%

commit v1 on v0

v1 whole, which is shorter than its diff:
```python
import functools
import math

import jax
import jax.numpy as jnp
from jax import lax
from jax.experimental import pallas as pl
from jax.experimental.pallas import tpu as pltpu
from jax.sharding import PartitionSpec as P

MESH = pl.DeviceIdType.MESH
BF16 = jnp.bfloat16
F32 = jnp.float32
VMEM_BYTES = 50 * 1024 * 1024


def greet_all(wide_count):
    me = lax.axis_index("wide") * 2 + lax.axis_index("narrow")
    total = 2 * wide_count
    barrier = pltpu.get_barrier_semaphore()

    def greet(k, carry):
        other = lax.rem(me + k, total)
        pl.semaphore_signal(
            barrier, inc=1, device_id={"wide": other // 2, "narrow": lax.rem(other, 2)}, device_id_type=MESH
        )
        return carry

    lax.fori_loop(1, total, greet, 0)
    pl.semaphore_wait(barrier, total - 1)


def remote(src, dst, send_sem, recv_sem, wide, narrow):
    return pltpu.make_async_remote_copy(
        src_ref=src,
        dst_ref=dst,
        send_sem=send_sem,
        recv_sem=recv_sem,
        device_id={"wide": wide, "narrow": narrow},
        device_id_type=MESH,
    )


def gather_kernel(W, tr, v_ref, g_ref, slab_ref, halo_ref, ssem, rsem, fssem, frsem, hs, hr, lsem):
    w = lax.axis_index("wide")
    n = lax.axis_index("narrow")
    half = tr + 2
    greet_all(W)
    place = 2 * n

    me = w * 2 + n
    nxt = lax.rem(me + 1, 2 * W)
    prv = lax.rem(me + 2 * W - 1, 2 * W)
    down = remote(g_ref.at[tr - 1], halo_ref.at[0], hs.at[0], hr.at[0], nxt // 2, lax.rem(nxt, 2))
    up = remote(g_ref.at[0], halo_ref.at[1], hs.at[1], hr.at[1], prv // 2, lax.rem(prv, 2))

    def outgoing(dst):
        return remote(
            v_ref.at[pl.ds(2 * tr * dst + half * n, half)],
            slab_ref.at[w, pl.ds(place, half)],
            ssem.at[dst],
            rsem.at[w],
            dst,
            n,
        )

    def forward(src):
        return remote(
            slab_ref.at[src, pl.ds(tr * (1 - n) + 2 * n, 2)],
            slab_ref.at[src, pl.ds(half * n, 2)],
            fssem.at[src],
            frsem.at[src],
            w,
            1 - n,
        )

    def start(k, carry):
        outgoing(lax.rem(w + k, W)).start()
        return carry

    lax.fori_loop(1, W, start, 0)
    own = pltpu.make_async_copy(
        v_ref.at[pl.ds(2 * tr * w + tr * n, tr + 4)], slab_ref.at[w], lsem
    )
    own.start()
    down.start()
    up.start()

    def relay(k, carry):
        src = lax.rem(w + W - k, W)
        remote(
            v_ref.at[pl.ds(0, half)], slab_ref.at[src, pl.ds(place, half)], ssem.at[src], rsem.at[src], src, n
        ).wait_recv()
        forward(src).start()
        return carry

    lax.fori_loop(1, W, relay, 0)
    own.wait()

    def finish(k, carry):
        src = lax.rem(w + W - k, W)
        fwd = remote(
            slab_ref.at[src, pl.ds(0, 2)],
            slab_ref.at[src, pl.ds(half * (1 - n), 2)],
            fssem.at[src],
            frsem.at[src],
            w,
            1 - n,
        )
        fwd.wait_recv()
        forward(src).wait_send()
        outgoing(src).wait_send()
        return carry

    lax.fori_loop(1, W, finish, 0)
    down.wait()
    up.wait()


def nt(a, b):
    return lax.dot_general(a, b, (((1,), (1,)), ((), ())), preferred_element_type=F32)


def compute_kernel(
    W, tr, F, T, taps, pscale, tscale,
    slab_ref, g_ref, halo_ref, ws_ref, sb_ref, wv_ref, wt_ref, tb_ref, we_ref, wo_ref,
    out_ref, gv_ref, gs_ref, gt_ref,
    stack, gpad, apad, gsum, tsum,
):
    cin = slab_ref.shape[2]
    cols = slab_ref.shape[3]
    cmid = ws_ref.shape[0]
    cout = wt_ref.shape[0]
    half = taps // 2
    gp_rows = tr + 2
    px = tr * cols
    lead = half // 2
    me = lax.axis_index("wide") * 2 + lax.axis_index("narrow")

    gpad[0 : lead * cout, :] = jnp.zeros((lead * cout, gp_rows * cols), BF16)
    gpad[(lead + T) * cout :, :] = jnp.zeros((lead * cout, gp_rows * cols), BF16)
    apad[0 : half * cmid, :] = jnp.zeros((half * cmid, px), BF16)
    apad[(half + F) * cmid :, :] = jnp.zeros((half * cmid, px), BF16)
    body = slice(lead * cout, (lead + T) * cout)
    above = halo_ref[0].reshape(T * cout, cols)
    gpad[body, 0:cols] = jnp.where(me == 0, jnp.zeros_like(above), above)
    for r in range(tr):
        gpad[body, (r + 1) * cols : (r + 2) * cols] = g_ref[r].reshape(T * cout, cols)
    below = halo_ref[1].reshape(T * cout, cols)
    gpad[body, (tr + 1) * cols :] = jnp.where(me == 2 * W - 1, jnp.zeros_like(below), below)

    gsum[...] = jnp.zeros_like(gsum)
    tsum[...] = jnp.zeros_like(tsum)
    rows6 = tr + 4
    lane = lax.broadcasted_iota(jnp.int32, (rows6 * cin, cols), 1)
    lane_out = lax.broadcasted_iota(jnp.int32, (cin, cols), 1)
    bias = sb_ref[...]

    def frame(f, taps_mat, k_rows, g_start):
        x = slab_ref[f].reshape(rows6 * cin, cols)
        xf = x.astype(F32)
        left = jnp.where(lane == 0, 0.0, pltpu.roll(xf, 1, 1)).astype(BF16)
        right = jnp.where(lane == cols - 1, 0.0, pltpu.roll(xf, cols - 1, 1)).astype(BF16)
        stack[:, 0] = left.reshape(rows6, cin, cols)
        stack[:, 1] = x.reshape(rows6, cin, cols)
        stack[:, 2] = right.reshape(rows6, cin, cols)
        big = jnp.concatenate(
            [stack[r : r + 3].reshape(9 * cin, cols) for r in range(gp_rows)], axis=1
        )
        pre = jnp.dot(ws_ref[...], big, preferred_element_type=F32) + bias
        s = 1.0 / (1.0 + jnp.exp(-pre))
        act = (pre[:, cols : cols + px] * s[:, cols : cols + px]).astype(BF16)
        apad[pl.ds(pl.multiple_of((f + half) * cmid, 16), cmid), :] = act
        ga = jnp.dot(
            taps_mat, gpad[pl.ds(pl.multiple_of(g_start, 16), k_rows), :], preferred_element_type=F32
        )
        slope = s * (1.0 + pre * (1.0 - s))
        gp = (ga.astype(BF16).astype(F32) * slope).astype(BF16)
        gsum[...] += nt(gp[:, cols : cols + px], big[:, cols : cols + px])
        tall = jnp.concatenate([gp[:, i * cols : i * cols + px] for i in range(3)], axis=0)
        z = jnp.dot(wv_ref[...], tall, preferred_element_type=F32)
        for r in range(tr):
            zr = z[:, r * cols : (r + 1) * cols]
            total = zr[cin : 2 * cin]
            total += jnp.where(lane_out == cols - 1, 0.0, pltpu.roll(zr[0:cin], cols - 1, 1))
            total += jnp.where(lane_out == 0, 0.0, pltpu.roll(zr[2 * cin :], 1, 1))
            gv_ref[f, r] = total.astype(BF16)

    def pair(q, carry):
        frame(2 * q, we_ref[...], we_ref.shape[1], q * cout)
        frame(2 * q + 1, wo_ref[...], wo_ref.shape[1], (q + 1) * cout)
        return carry

    lax.fori_loop(0, F // 2, pair, 0)

    def step(t, carry):
        a = apad[pl.ds(pl.multiple_of(2 * t * cmid, 16), taps * cmid), :]
        o = jnp.dot(wt_ref[...], a, preferred_element_type=F32) + tb_ref[...]
        out_ref[t] = o.astype(BF16)
        g = gpad[pl.ds(pl.multiple_of((t + lead) * cout, 16), cout), cols : cols + px]
        tsum[...] += nt(g, a)
        return carry

    lax.fori_loop(0, T, step, 0)
    gs_ref[...] = gsum[...] * pscale
    gt_ref[...] = tsum[...] * tscale


def reduce_kernel(W, tr, part_ref, gv_ref, full_ref, gvr_ref,
                  nrecv, sbuf, rbuf, ns, nr, rs_s, rs_r, ag_s, ag_r, fw_s, fw_r, gv_s, gv_r, lsem):
    w = lax.axis_index("wide")
    n = lax.axis_index("narrow")
    per = W // 2
    goal = w // per
    greet_all(W)
    swap = remote(part_ref.at[1 - n], nrecv, ns, nr, w, 1 - n)
    swap.start()
    spot = lax.rem(w, per) * 2 + n

    def gv_copy(f):
        return remote(gv_ref.at[f], gvr_ref.at[pl.ds(spot * tr, tr)], gv_s.at[f], gv_r.at[spot], f, goal)

    swap.wait_recv()
    sbuf[...] = (part_ref[n] + nrecv[...]).astype(BF16)

    def rs_copy(dst):
        return remote(sbuf.at[dst], rbuf.at[w], rs_s.at[dst], rs_r.at[w], dst, n)

    def start_rs(k, carry):
        rs_copy(lax.rem(w + k, W)).start()
        return carry

    lax.fori_loop(1, W, start_rs, 0)

    def start_gv(k, carry):
        gv_copy(lax.rem(w + k, W)).start()
        return carry

    lax.fori_loop(1, W, start_gv, 0)

    mine = pltpu.make_async_copy(gv_ref.at[w], gvr_ref.at[pl.ds(spot * tr, tr)], lsem)

    @pl.when(goal == n)
    def _():
        mine.start()

    @pl.when(goal != n)
    def _():
        gv_copy(w).start()

    rbuf[w] = sbuf[w]

    def wait_rs(k, carry):
        src = lax.rem(w + W - k, W)
        remote(sbuf.at[src], rbuf.at[src], rs_s.at[src], rs_r.at[src], src, n).wait_recv()
        return carry

    lax.fori_loop(1, W, wait_rs, 0)
    full_ref[n, w] = jnp.sum(rbuf[...].astype(F32), axis=0).astype(BF16)

    def ag_copy(dst):
        return remote(full_ref.at[n, w], full_ref.at[n, w], ag_s.at[dst], ag_r.at[w], dst, n)

    def start_ag(k, carry):
        ag_copy(lax.rem(w + k, W)).start()
        return carry

    lax.fori_loop(1, W, start_ag, 0)

    def fw_copy(src):
        return remote(full_ref.at[n, src], full_ref.at[n, src], fw_s.at[src], fw_r.at[src], w, 1 - n)

    fw_copy(w).start()

    def relay(k, carry):
        src = lax.rem(w + W - k, W)
        remote(full_ref.at[n, src], full_ref.at[n, src], ag_s.at[src], ag_r.at[src], src, n).wait_recv()
        fw_copy(src).start()
        return carry

    lax.fori_loop(1, W, relay, 0)

    first = per * 2 * n
    me = w * 2 + n

    def wait_gv(i, carry):
        @pl.when(first + i != me)
        def _():
            remote(
                gv_ref.at[0], gvr_ref.at[pl.ds(i * tr, tr)], gv_s.at[0], gv_r.at[i], w, 1 - n
            ).wait_recv()

        return carry

    lax.fori_loop(0, 2 * per, wait_gv, 0)

    def finish(k, carry):
        other = lax.rem(w + k, W)
        rs_copy(other).wait_send()
        ag_copy(other).wait_send()
        gv_copy(other).wait_send()
        return carry

    lax.fori_loop(1, W, finish, 0)

    def finish_fw(s, carry):
        remote(
            full_ref.at[1 - n, s], full_ref.at[1 - n, s], fw_s.at[s], fw_r.at[s], w, 1 - n
        ).wait_recv()
        fw_copy(s).wait_send()
        return carry

    lax.fori_loop(0, W, finish_fw, 0)
    swap.wait_send()

    @pl.when(goal == n)
    def _():
        mine.wait()

    @pl.when(goal != n)
    def _():
        gv_copy(w).wait_send()


def per_device(video, spatial_weight, spatial_bias, temporal_weight, temporal_bias, out_cotangent):
    W = lax.axis_size("wide")
    _, cin, R, cols = video.shape
    cmid = spatial_weight.shape[0]
    cout, taps, _ = temporal_weight.shape
    T = out_cotangent.shape[0]
    tr = out_cotangent.shape[2]
    F = W
    px = tr * cols
    half = taps // 2
    tscale = 1.0 / math.sqrt(T * R * cols)
    pscale = 1.0 / math.sqrt(F * R * cols)
    dma = pltpu.SemaphoreType.DMA
    hbm = pl.BlockSpec(memory_space=pl.ANY)
    vmem = pl.BlockSpec(memory_space=pltpu.VMEM)

    v_rows = jnp.pad(jnp.transpose(video[0], (1, 0, 2)), ((2, 2), (0, 0), (0, 0)))
    g_rows = jnp.transpose(out_cotangent, (2, 0, 1, 3))
    slab, halo = pl.pallas_call(
        functools.partial(gather_kernel, W, tr),
        out_shape=(
            jax.ShapeDtypeStruct((F, tr + 4, cin, cols), BF16),
            jax.ShapeDtypeStruct((2, T, cout, cols), BF16),
        ),
        in_specs=[hbm, hbm],
        out_specs=(hbm, hbm),
        scratch_shapes=[dma((W,)), dma((W,)), dma((W,)), dma((W,)), dma((2,)), dma((2,)), dma],
        compiler_params=pltpu.CompilerParams(collective_id=0, has_side_effects=True),
        name="gather_rows",
    )(v_rows, g_rows)

    ws = spatial_weight.reshape(cmid, 9 * cin)
    grid_w = spatial_weight.reshape(cmid, 3, 3, cin)[:, ::-1]
    wv = jnp.transpose(grid_w, (2, 3, 1, 0)).reshape(3 * cin, 3 * cmid)
    wt = temporal_weight.reshape(cout, taps * cmid)
    rev = jnp.transpose(temporal_weight[:, ::-1], (2, 1, 0))
    we = rev[:, 0::2].reshape(cmid, -1)
    wo = rev[:, 1::2].reshape(cmid, -1)

    out, gv, gs, gt = pl.pallas_call(
        functools.partial(compute_kernel, W, tr, F, T, taps, pscale, tscale),
        out_shape=(
            jax.ShapeDtypeStruct((T, cout, px), BF16),
            jax.ShapeDtypeStruct((F, tr, cin, cols), BF16),
            jax.ShapeDtypeStruct((cmid, 9 * cin), F32),
            jax.ShapeDtypeStruct((cout, taps * cmid), F32),
        ),
        in_specs=[vmem] * 10,
        out_specs=(vmem,) * 4,
        scratch_shapes=[
            pltpu.VMEM((tr + 4, 3, cin, cols), BF16),
            pltpu.VMEM(((T + half) * cout, (tr + 2) * cols), BF16),
            pltpu.VMEM(((F + 2 * half) * cmid, px), BF16),
            pltpu.VMEM((cmid, 9 * cin), F32),
            pltpu.VMEM((cout, taps * cmid), F32),
        ],
        compiler_params=pltpu.CompilerParams(vmem_limit_bytes=VMEM_BYTES),
        name="block_compute",
    )(slab, g_rows, halo, ws, spatial_bias[:, None], wv, wt, temporal_bias[:, None], we, wo)

    size_s = cmid * 9 * cin // 2
    size_t = cout * taps * cmid // 2
    rows = -(-(size_s + size_t) // (W * 128 * 16)) * 16
    flat = jnp.concatenate([gs.reshape(2, size_s), gt.reshape(2, size_t)], axis=1)
    flat = jnp.pad(flat, ((0, 0), (0, W * rows * 128 - size_s - size_t)))
    full, gv_rows = pl.pallas_call(
        functools.partial(reduce_kernel, W, tr),
        out_shape=(
            jax.ShapeDtypeStruct((2, W, rows, 128), BF16),
            jax.ShapeDtypeStruct((R // 2, cin, cols), BF16),
        ),
        in_specs=[vmem, hbm],
        out_specs=(vmem, hbm),
        scratch_shapes=[
            pltpu.VMEM((W, rows, 128), F32),
            pltpu.VMEM((W, rows, 128), BF16),
            pltpu.VMEM((W, rows, 128), BF16),
            dma, dma, dma((W,)), dma((W,)), dma((W,)), dma((W,)), dma((W,)), dma((W,)), dma((W,)), dma((W,)), dma,
        ],
        compiler_params=pltpu.CompilerParams(
            collective_id=1, has_side_effects=True, vmem_limit_bytes=VMEM_BYTES
        ),
        name="reduce_and_return",
    )(flat.reshape(2, W, rows, 128), gv)

    full = full.reshape(2, W * rows * 128)
    own = lax.dynamic_index_in_dim(full, lax.axis_index("narrow"), 0, keepdims=False)
    grad_spatial = own[:size_s].reshape(cmid // 2, 9, cin).astype(F32)
    grad_temporal = full[:, size_s : size_s + size_t].reshape(cout, taps, cmid).astype(F32)
    grad_video = jnp.transpose(gv_rows, (1, 0, 2))[None]
    output = out.reshape(T, cout, tr, cols)
    return (output, grad_video, grad_spatial, grad_temporal)


def solution(mesh):
    in_specs = (
        P(("grp", "wide"), None, None, None),
        P(),
        P(),
        P(),
        P(),
        P("grp", None, ("wide", "narrow"), None),
    )
    out_specs = (
        P("grp", None, ("wide", "narrow"), None),
        P(("grp", "wide"), None, "narrow", None),
        P(("grp", "narrow"), None, None),
        P("grp", None, None),
    )
    return jax.shard_map(
        per_device, mesh=mesh, in_specs=in_specs, out_specs=out_specs, check_vma=False
    )
```

time: 238 us -> 65.7 us (0.28)
  waiting for transfers between devices: 167 us -> 0 us
  Pallas kernels: 0 us -> 49.2 us
  between operations: 16 us -> 0.85 us
  matrix products: 13.8 us -> 0 us
  starting transfers between devices: 11 us -> 0 us
  blocking collectives: 8.55 us -> 0 us
  local copies, waits for them, and re-layouts: 18.9 us -> 14.5 us
    psum x2 -> x0, waiting for transfers between devices: 145 us -> none  [the longest x1 94.1 us: per_device(): lax.psum(local_temporal * temporal_scale, ('wide', 'narrow'))]
    pallas_call x0 -> x3, Pallas kernels: none -> 49.2 us  [the longest x1 24.9 us: per_device(): pl.pallas_call(functools.partial(reduce_kernel, W, tr), out_shape=(jax.Sh...]
    all_to_all x2 -> x0, waiting for transfers between devices: 22.2 us -> none  [the longest x1 11.4 us: per_device(): lax.all_to_all(sectioned, 'wide', split_axis=2, concat_axis=0, tiled=True)]
    dot_general x12 -> x0, matrix products: 13.8 us -> none  [the longest x3 5.12 us: spatial_forward(): jnp.einsum('ojc,fjcyx->foyx', weights_grid[:, row_shift], slab_list[row_s...]
    all_to_all x2 -> x0, starting transfers between devices: 10.9 us -> none  [the longest x1 7.28 us: per_device(): lax.all_to_all(split_cores, 'wide', split_axis=0, concat_axis=2, tiled=True)]
    all_to_all x2 -> x0, blocking collectives: 8.55 us -> none  [the longest x1 4.34 us: per_device(): lax.all_to_all(shaped, 'narrow', split_axis=1, concat_axis=3, tiled=True)]
    another operation x6 -> x0, local copies, waits for them, and re-layouts: 4.19 us -> none  [the longest x2 3.09 us: shifted_slabs(): slab_list.append(jnp.stack(pieces, axis=1))]
    unnamed x54 -> x22, local copies, waits for them, and re-layouts: 7.54 us -> 8.67 us
  transfers between devices with their start and end apart: 5 -> 0, of which waited for: 4 -> 0; matrix products, arithmetic and copies ran while one was open for 7% -> 0% of each run, Pallas kernels for 0% -> 0%
where the time goes in v1:
time: 65.7 us; the launch traced here: 65.4 us
  Pallas kernels  49.2 us (75%)
  local copies, waits for them, and re-layouts  14.5 us (22%)
  other arithmetic  0.92 us (1%)
  between operations  0.85 us (1%)
    pallas_call x1, Pallas kernels, per_device(): pl.pallas_call(functools.partial(reduce_kernel, W, tr), out_shape=(jax.Sh...  24.9 us
    pallas_call x1, Pallas kernels, per_device(): pl.pallas_call(functools.partial(gather_kernel, W, tr), out_shape=(jax.Sh...  17.5 us
    unnamed x22, local copies, waits for them, and re-layouts  8.67 us
    pallas_call x1, Pallas kernels, per_device(): pl.pallas_call(functools.partial(compute_kernel, W, tr, F, T, taps, pscal...  6.81 us
    rev x1, local copies, waits for them, and re-layouts, per_device(): grid_w = spatial_weight.reshape(cmid, 3, 3, cin)[:, ::-1]  1.62 us

profile of v1, /device:TPU:0, one launch (start us, length us, event | category | flops | bytes accessed | tf_op | source)
XLA Modules:
  0.0 65.4 jit_solution(17446836425183449893)
XLA Ops:
  0.6 1.6 %copy.40 = bf16[4,64,2,128]{3,1,0,2:T(8,128)(2,1)} copy(bf16[4,64,2,128]{3,2,1,0:T(2,128)(2,1)} %param.11) | data formatting | bytes 262144 | tf_op args[5]
  2.2 1.2 %copy.38 = bf16[1,64,32,128]{3,1,2,0:T(8,128)(2,1)S(1)} copy(bf16[1,64,32,128]{3,2,1,0:T(8,128)(2,1)} %param.6) | data formatting | bytes 1048576 | tf_op args[0]
  3.5 0.9 %pad.8.v_ref = bf16[36,64,128]{2,1,0:T(8,128)(2,1)} pad(bf16[32,64,128]{2,1,0:T(8,128)(2,1)S(1)} %bitcast.35, bf16[]{:T(256)} %constant.10.clone.1), padding=2_2x0_0x0_0 | pad | bytes 1114114 | tf_op jit(solution)/shard_map/jit(_pad)/pad | solution.py:341
  4.3 17.5 %gather_rows.1 = (bf16[8,6,64,128]{3,2,1,0:T(8,128)(2,1)}, bf16[2,4,64,128]{3,2,1,0:T(8,128)(2,1)}) custom-call(bf16[36,64,128]{2,1,0:T(8,128)(2,1)} %pad.8.v_ref, bf16[2,4,64,128]{3,2,1,0:T(8,128)(2,1)} %bitcast.31), custom_call_target="tpu_custom_call" | custom-call | tf_op jit(solution)/shard_map/gather_rows/pallas_call | solution.py:343
  21.9 0.1 copy.28.we_ref
  22.0 0.1 copy.32.wo_ref
  22.1 0.8 %copy-done.4 = bf16[144,9,64]{0,2,1:T(8,128)(2,1)S(1)} copy-done((bf16[144,9,64]{0,2,1:T(8,128)(2,1)S(1)}, bf16[144,9,64]{0,2,1:T(8,128)(2,1)}, u32[]{:S(2)}) %copy-start.4) | copy-done | bytes 165912
  23.0 0.3 copy.21
  23.2 1.6 %rev.6 = bf16[144,3,3,64]{0,1,3,2:T(4,128)(2,1)S(1)} reverse(bf16[144,3,3,64]{0,1,3,2:T(4,128)(2,1)S(1)} %copy.21), dimensions={1} | reverse | bytes 331776 | tf_op jit(solution)/shard_map/rev | solution.py:357
  24.9 0.2 reshape.51.wv_ref
  25.1 0.3 copy.22
  25.4 0.2 copy.26.wt_ref
  25.6 0.2 copy.24.ws_ref
  25.7 0.7 %copy-done.5 = f32[144]{0:T(256)S(1)} copy-done((f32[144]{0:T(256)S(1)}, f32[144]{0:T(256)}, u32[]{:S(2)}) %copy-start.5) | copy-done | bytes 600
  26.4 0.1 copy.25.sb_ref
  26.5 0.7 copy-done.6
  27.2 0.1 copy.27.tb_ref
  27.3 6.8 %block_compute.1 = (bf16[4,64,256]{2,1,0:T(8,128)(2,1)S(1)}, bf16[8,2,64,128]{3,2,1,0:T(8,128)(2,1)S(1)}, f32[144,576]{1,0:T(8,128)S(1)}, f32[64,1296]{1,0:T(8,128)S(1)}) custom-call(bf16[8,6,64,128]{3,2,1,0:T(8,128)(2,1)S(1)} %copy-done.1, bf16[2,4,64,128]{3,2,1,0:T(8,128)(2,1)S(1)} %bitcast.32, bf16[2,4,64,128]{3,2,1,0:T(8,128)(2,1)S(1)} %copy-done.2, ...), custom_call_target="tpu_custom_call" | custom-call | tf_op jit(solution)/shard_map/block_compute/pallas_call | solution.py:364
  34.1 0.3 reshape.56
  34.4 0.5 reshape.57
  34.9 0.3 fusion
  35.2 0.1 copy.33
  35.3 24.9 %reduce_and_return.1 = (bf16[2,8,96,128]{3,2,1,0:T(8,128)(2,1)S(1)}, bf16[16,64,128]{2,1,0:T(8,128)(2,1)S(1)}) custom-call(f32[2,8,96,128]{3,2,1,0:T(8,128)S(1)} %bitcast.30, bf16[8,2,64,128]{3,2,1,0:T(8,128)(2,1)S(1)} %get-tuple-element.17.gv_ref), custom_call_target="tpu_custom_call" | custom-call | tf_op jit(solution)/shard_map/reduce_and_return/pallas_call | solution.py:390
  60.2 0.4 copy.39
  60.6 0.5 fusion.1
  61.1 0.1 reshape.60
  61.2 0.9 %copy.30 = f32[72,9,64]{0,2,1:T(8,128)} copy(f32[72,9,64]{2,1,0:T(8,128)S(1)} %reshape.60) | data formatting | bytes 331776
  62.2 0.1 slice_convert_fusion
  62.3 0.4 reshape.61
  62.7 1.2 %copy.31 = f32[64,9,144]{2,0,1:T(8,128)} copy(f32[64,9,144]{2,1,0:T(8,128)S(1)} %reshape.61) | data formatting | bytes 663552
  63.9 0.9 %copy.29 = bf16[1,64,16,128]{3,2,1,0:T(8,128)(2,1)} copy(bf16[1,64,16,128]{3,1,2,0:T(8,128)(2,1)S(1)} %bitcast.34) | data formatting | bytes 524288
  64.7 0.7 %reshape.55 = bf16[4,64,2,128]{3,2,1,0:T(2,128)(2,1)} reshape(bf16[4,64,256]{2,1,0:T(8,128)(2,1)S(1)} %get-tuple-element.14) | data formatting | bytes 262144 | tf_op jit(solution)/shard_map/reshape | solution.py:415
  (14 shorter events, 0.1 us)
Async XLA Ops:
  4.3 17.5 %copy-start.3 = (bf16[64,9,144]{2,0,1:T(8,128)(2,1)S(1)}, bf16[64,9,144]{2,0,1:T(8,128)(2,1)}, u32[]{:S(2)}) copy-start(bf16[64,9,144]{2,0,1:T(8,128)(2,1)} %param.9) | copy-start | bytes 497668
  22.0 1.0 %copy-start.4 = (bf16[144,9,64]{0,2,1:T(8,128)(2,1)S(1)}, bf16[144,9,64]{0,2,1:T(8,128)(2,1)}, u32[]{:S(2)}) copy-start(bf16[144,9,64]{0,2,1:T(8,128)(2,1)} %param.7) | copy-start | bytes 497668
  25.1 2.2 %copy-start.1 = (bf16[8,6,64,128]{3,2,1,0:T(8,128)(2,1)S(1)}, bf16[8,6,64,128]{3,2,1,0:T(8,128)(2,1)}, u32[]{:S(2)}) copy-start(bf16[8,6,64,128]{3,2,1,0:T(8,128)(2,1)} %get-tuple-element.12.slab_ref) | copy-start | bytes 2359300
  25.5 1.7 %copy-start = (bf16[4,64,2,128]{3,1,0,2:T(8,128)(2,1)S(1)}, bf16[4,64,2,128]{3,1,0,2:T(8,128)(2,1)}, u32[]{:S(2)}) copy-start(bf16[4,64,2,128]{3,1,0,2:T(8,128)(2,1)} %copy.40) | copy-start | bytes 393220
  25.5 1.7 %copy-start.2 = (bf16[2,4,64,128]{3,2,1,0:T(8,128)(2,1)S(1)}, bf16[2,4,64,128]{3,2,1,0:T(8,128)(2,1)}, u32[]{:S(2)}) copy-start(bf16[2,4,64,128]{3,2,1,0:T(8,128)(2,1)} %get-tuple-element.13.halo_ref) | copy-start | bytes 393220
  25.7 0.7 %copy-start.5 = (f32[144]{0:T(256)S(1)}, f32[144]{0:T(256)}, u32[]{:S(2)}) copy-start(f32[144]{0:T(256)} %param.8) | copy-start | bytes 1732
  26.5 0.7 %copy-start.6 = (f32[64]{0:T(128)S(1)}, f32[64]{0:T(128)}, u32[]{:S(2)}) copy-start(f32[64]{0:T(128)} %param.10) | copy-start | bytes 772

commit v2 on v1

v2 whole, which is shorter than its diff:
```python
import functools
import math

import jax
import jax.numpy as jnp
from jax import lax
from jax.experimental import pallas as pl
from jax.experimental.pallas import tpu as pltpu
from jax.sharding import PartitionSpec as P

MESH = pl.DeviceIdType.MESH
BF16 = jnp.bfloat16
F32 = jnp.float32
VMEM_BYTES = 50 * 1024 * 1024


def greet_all(wide_count):
    me = lax.axis_index("wide") * 2 + lax.axis_index("narrow")
    total = 2 * wide_count
    barrier = pltpu.get_barrier_semaphore()

    def greet(k, carry):
        other = lax.rem(me + k, total)
        pl.semaphore_signal(
            barrier, inc=1, device_id={"wide": other // 2, "narrow": lax.rem(other, 2)}, device_id_type=MESH
        )
        return carry

    lax.fori_loop(1, total, greet, 0)
    pl.semaphore_wait(barrier, total - 1)


def remote(src, dst, send_sem, recv_sem, wide, narrow):
    return pltpu.make_async_remote_copy(
        src_ref=src,
        dst_ref=dst,
        send_sem=send_sem,
        recv_sem=recv_sem,
        device_id={"wide": wide, "narrow": narrow},
        device_id_type=MESH,
    )


def nt(a, b):
    return lax.dot_general(a, b, (((1,), (1,)), ((), ())), preferred_element_type=F32)


def fold_lanes(x):
    rows, lanes = x.shape
    blocks = lanes // 128
    parts = [x[:, 128 * b : 128 * (b + 1)] for b in range(blocks)]
    left = lanes - 128 * blocks
    if not left:
        return parts, []
    fold = 128 // left
    piece = rows // fold
    last = jnp.concatenate([x[piece * i : piece * (i + 1), 128 * blocks :] for i in range(fold)], axis=1)
    return parts, [last]


def unfold_lanes(parts, last, lanes):
    blocks = lanes // 128
    left = lanes - 128 * blocks
    if not left:
        return jnp.concatenate(parts, axis=1)
    fold = 128 // left
    end = jnp.concatenate([last[:, left * i : left * (i + 1)] for i in range(fold)], axis=0)
    return jnp.concatenate(parts + [end], axis=1)


def block_kernel(
    W, tr, T, taps, rows, pscale, tscale,
    v_ref, g_ref, ws_ref, sb_ref, wt_ref, tb_ref,
    out_ref, gvr_ref, gs_ref, gt_ref,
    vpad, slab, halo, stack, gpad, apad, gsum, tsum, wv, wtap, gv,
    nrs, nrt, sbuf, rbuf, full,
    v_s, v_r, vf_s, vf_r, h_s, h_r, ns, nr, rs_s, rs_r, ag_s, ag_r, fw_s, fw_r, gv_s, gv_r, lsem,
):
    F = W
    w = lax.axis_index("wide")
    n = lax.axis_index("narrow")
    me = w * 2 + n
    R, cin, cols = v_ref.shape
    cmid = ws_ref.shape[0]
    cout = wt_ref.shape[0]
    half = taps // 2
    lead = half // 2
    gp_rows = tr + 2
    px = tr * cols
    rows6 = tr + 4
    got = tr + 2
    even_taps = half + 1
    per = W // 2
    goal = w // per
    spot = lax.rem(w, per) * 2 + n
    low_tap = 2 * (T - 1) - half
    place = 2 * n

    vpad[0:2] = jnp.zeros((2, cin, cols), BF16)
    vpad[R + 2 :] = jnp.zeros((2, cin, cols), BF16)
    vpad[2 : R + 2] = v_ref[...]
    greet_all(W)

    nxt = lax.rem(me + 1, 2 * W)
    prv = lax.rem(me + 2 * W - 1, 2 * W)
    down = remote(g_ref.at[tr - 1], halo.at[0], h_s.at[0], h_r.at[0], nxt // 2, lax.rem(nxt, 2))
    up = remote(g_ref.at[0], halo.at[1], h_s.at[1], h_r.at[1], prv // 2, lax.rem(prv, 2))
    down.start()
    up.start()

    def v_copy(dst):
        return remote(
            vpad.at[pl.ds(2 * tr * dst + got * n, got)], slab.at[w, pl.ds(place, got)], v_s.at[dst], v_r.at[w], dst, n
        )

    def v_arrival(src):
        return remote(
            vpad.at[pl.ds(0, got)], slab.at[src, pl.ds(place, got)], v_s.at[src], v_r.at[src], src, n
        )

    def v_forward(src):
        return remote(
            slab.at[src, pl.ds(tr * (1 - n) + 2 * n, 2)], slab.at[src, pl.ds(got * n, 2)],
            vf_s.at[src], vf_r.at[src], w, 1 - n,
        )

    def v_forwarded(src):
        return remote(
            slab.at[src, pl.ds(0, 2)], slab.at[src, pl.ds(got * (1 - n), 2)], vf_s.at[src], vf_r.at[src], w, 1 - n
        )

    def gv_copy(f):
        return remote(gv.at[f], gvr_ref.at[pl.ds(spot * tr, tr)], gv_s.at[f], gv_r.at[spot], f, goal)

    mine = pltpu.make_async_copy(gv.at[w], gvr_ref.at[pl.ds(spot * tr, tr)], lsem)

    def start(k, carry):
        v_copy(lax.rem(w + k, W)).start()
        return carry

    lax.fori_loop(1, W, start, 0)

    slab[w] = vpad[pl.ds(2 * tr * w + tr * n, rows6)]
    for i in range(3):
        wv[i] = ws_ref[:, 3 * cin * i : 3 * cin * (i + 1)].astype(F32).T.astype(BF16)
    for parity in range(2):
        for m in range(even_taps):
            k = taps - 1 - parity - 2 * m
            spread = slice(m * cout, (m + 1) * cout)
            if k < 0:
                wtap[parity, :, spread] = jnp.zeros((cmid, cout), BF16)
            else:
                wtap[parity, :, spread] = wt_ref[:, k * cmid : (k + 1) * cmid].astype(F32).T.astype(BF16)
    gpad[0 : lead * cout, :] = jnp.zeros((lead * cout, gp_rows * cols), BF16)
    gpad[(lead + T) * cout :, :] = jnp.zeros(((lead + 1) * cout, gp_rows * cols), BF16)
    apad[0 : half * cmid, :] = jnp.zeros((half * cmid, px), BF16)
    apad[(half + F) * cmid :, :] = jnp.zeros((half * cmid, px), BF16)
    gsum[...] = jnp.zeros_like(gsum)
    tsum[...] = jnp.zeros_like(tsum)

    body = slice(lead * cout, (lead + T) * cout)
    for r in range(tr):
        gpad[body, (r + 1) * cols : (r + 2) * cols] = g_ref[r].reshape(T * cout, cols)
    down.wait_recv()
    up.wait_recv()
    above = halo[0].reshape(T * cout, cols)
    gpad[body, 0:cols] = jnp.where(me == 0, jnp.zeros_like(above), above)
    below = halo[1].reshape(T * cout, cols)
    gpad[body, (tr + 1) * cols :] = jnp.where(me == 2 * W - 1, jnp.zeros_like(below), below)

    lane = lax.broadcasted_iota(jnp.int32, (rows6 * cin, cols), 1)
    lane_out = lax.broadcasted_iota(jnp.int32, (cin, cols), 1)

    def frame(f):
        x = slab[f].reshape(rows6 * cin, cols)
        xf = x.astype(F32)
        left = jnp.where(lane == 0, 0.0, pltpu.roll(xf, 1, 1)).astype(BF16)
        right = jnp.where(lane == cols - 1, 0.0, pltpu.roll(xf, cols - 1, 1)).astype(BF16)
        stack[:, 0] = left.reshape(rows6, cin, cols)
        stack[:, 1] = x.reshape(rows6, cin, cols)
        stack[:, 2] = right.reshape(rows6, cin, cols)
        big = jnp.concatenate(
            [stack[r : r + 3].reshape(9 * cin, cols) for r in range(gp_rows)], axis=1
        )
        pre = jnp.dot(ws_ref[...], big, preferred_element_type=F32) + sb_ref[...]
        s = 1.0 / (1.0 + jnp.exp(-pre))
        act = (pre[:, cols : cols + px] * s[:, cols : cols + px]).astype(BF16)
        apad[pl.ds(pl.multiple_of((f + half) * cmid, 16), cmid), :] = act
        odd = lax.rem(f, 2)
        g_start = pl.multiple_of((f // 2 + odd) * cout, 16)
        ga = jnp.dot(wtap[odd], gpad[pl.ds(g_start, even_taps * cout), :], preferred_element_type=F32)
        slope = s * (1.0 + pre * (1.0 - s))
        gp = (ga.astype(BF16).astype(F32) * slope).astype(BF16)
        z = jnp.dot(wv[2], gp[:, 0:px], preferred_element_type=F32)
        z += jnp.dot(wv[1], gp[:, cols : cols + px], preferred_element_type=F32)
        z += jnp.dot(wv[0], gp[:, 2 * cols : 2 * cols + px], preferred_element_type=F32)
        for r in range(tr):
            zr = z[:, r * cols : (r + 1) * cols]
            total = zr[cin : 2 * cin]
            total += jnp.where(lane_out == cols - 1, 0.0, pltpu.roll(zr[0:cin], cols - 1, 1))
            total += jnp.where(lane_out == 0, 0.0, pltpu.roll(zr[2 * cin :], 1, 1))
            gv[f, r] = total.astype(BF16)
        gsum[...] += nt(gp[:, cols : cols + px], big[:, cols : cols + px])
        pairs = nt(gpad[body, cols : cols + px], act)
        for t in range(T):
            at = f + 2 * (T - 1 - t)
            tsum[at] += pairs[t * cout : (t + 1) * cout]

    frame(w)

    @pl.when(goal == n)
    def _():
        mine.start()

    @pl.when(goal != n)
    def _():
        gv_copy(w).start()

    v_arrival(lax.rem(w + W - 1, W)).wait_recv()
    v_forward(lax.rem(w + W - 1, W)).start()

    def each(k, carry):
        src = lax.rem(w + W - k, W)
        after = lax.rem(w + W - k - 1, W)

        @pl.when(k < W - 1)
        def _():
            v_arrival(after).wait_recv()
            v_forward(after).start()

        v_forwarded(src).wait_recv()
        frame(src)
        gv_copy(src).start()
        return carry

    lax.fori_loop(1, W, each, 0)

    hs, ht = cmid // 2, cout // 2

    def half_of(ref, size, which):
        return ref.at[pl.ds(pl.multiple_of(which * size, 8), size)]

    def tap_half(which):
        return tsum.at[pl.ds(low_tap, taps), pl.ds(pl.multiple_of(which * ht, 8), ht)]

    swap_s = remote(half_of(gsum, hs, 1 - n), nrs, ns.at[0], nr.at[0], w, 1 - n)
    swap_t = remote(tap_half(1 - n), nrt, ns.at[1], nr.at[1], w, 1 - n)
    swap_s.start()
    swap_t.start()
    swap_s.wait_recv()
    swap_t.wait_recv()
    mine_s = (gsum[pl.ds(pl.multiple_of(n * hs, 8), hs), :] + nrs[...]) * pscale
    mine_t = (tsum[pl.ds(low_tap, taps), pl.ds(pl.multiple_of(n * ht, 8), ht), :] + nrt[...]) * tscale
    main_s, last_s = fold_lanes(mine_s)
    main_t, last_t = fold_lanes(mine_t.reshape(taps * ht, cmid))
    flat = jnp.concatenate(main_s + main_t + last_s + last_t, axis=0)
    used = flat.shape[0]
    flat = jnp.concatenate([flat, jnp.zeros((W * rows - used, 128), F32)], axis=0)
    sbuf[...] = flat.astype(BF16)

    def chunk(i):
        return pl.ds(pl.multiple_of(i * rows, 16), rows)

    def rs_copy(dst):
        return remote(sbuf.at[chunk(dst)], rbuf.at[w], rs_s.at[dst], rs_r.at[w], dst, n)

    def start_rs(k, carry):
        rs_copy(lax.rem(w + k, W)).start()
        return carry

    lax.fori_loop(1, W, start_rs, 0)
    rbuf[w] = sbuf[chunk(w), :]

    def step(t, carry):
        a = apad[pl.ds(pl.multiple_of(2 * t * cmid, 16), taps * cmid), :]
        o = jnp.dot(wt_ref[...], a, preferred_element_type=F32) + tb_ref[...]
        out_ref[t] = o.astype(BF16)
        return carry

    lax.fori_loop(0, T, step, 0)

    def wait_rs(k, carry):
        src = lax.rem(w + W - k, W)
        remote(sbuf.at[chunk(src)], rbuf.at[src], rs_s.at[src], rs_r.at[src], src, n).wait_recv()
        return carry

    lax.fori_loop(1, W, wait_rs, 0)
    full[n, chunk(w), :] = jnp.sum(rbuf[...].astype(F32), axis=0).astype(BF16)

    def ag_copy(dst):
        return remote(full.at[n, chunk(w)], full.at[n, chunk(w)], ag_s.at[dst], ag_r.at[w], dst, n)

    def start_ag(k, carry):
        ag_copy(lax.rem(w + k, W)).start()
        return carry

    lax.fori_loop(1, W, start_ag, 0)

    def fw_copy(src):
        return remote(full.at[n, chunk(src)], full.at[n, chunk(src)], fw_s.at[src], fw_r.at[src], w, 1 - n)

    fw_copy(w).start()

    def relay(k, carry):
        src = lax.rem(w + W - k, W)
        remote(full.at[n, chunk(src)], full.at[n, chunk(src)], ag_s.at[src], ag_r.at[src], src, n).wait_recv()
        fw_copy(src).start()
        return carry

    lax.fori_loop(1, W, relay, 0)

    first = per * 2 * n

    def wait_gv(i, carry):
        @pl.when(first + i != me)
        def _():
            remote(gv.at[0], gvr_ref.at[pl.ds(i * tr, tr)], gv_s.at[0], gv_r.at[i], w, 1 - n).wait_recv()

        return carry

    lax.fori_loop(0, 2 * per, wait_gv, 0)

    def finish(k, carry):
        other = lax.rem(w + k, W)
        v_copy(other).wait_send()
        v_forward(other).wait_send()
        rs_copy(other).wait_send()
        ag_copy(other).wait_send()
        gv_copy(other).wait_send()
        return carry

    lax.fori_loop(1, W, finish, 0)

    def finish_fw(s, carry):
        remote(
            full.at[1 - n, chunk(s)], full.at[1 - n, chunk(s)], fw_s.at[s], fw_r.at[s], w, 1 - n
        ).wait_recv()
        fw_copy(s).wait_send()
        return carry

    lax.fori_loop(0, W, finish_fw, 0)
    down.wait_send()
    up.wait_send()
    swap_s.wait_send()
    swap_t.wait_send()

    @pl.when(goal == n)
    def _():
        mine.wait()

    @pl.when(goal != n)
    def _():
        gv_copy(w).wait_send()

    def spans(base, count, size):
        return [slice(base + i * size, base + (i + 1) * size) for i in range(count)]

    ns_blocks, nt_blocks = len(main_s), len(main_t)
    base_t = ns_blocks * hs
    base_ls = base_t + nt_blocks * taps * ht
    base_lt = base_ls + (last_s[0].shape[0] if last_s else 0)
    whole = full[n].astype(F32)
    gs_ref[...] = unfold_lanes(
        [whole[c] for c in spans(0, ns_blocks, hs)], whole[base_ls:base_lt], ws_ref.shape[1]
    )
    for h in range(2):
        whole = full[h].astype(F32)
        taps_h = unfold_lanes(
            [whole[c] for c in spans(base_t, nt_blocks, taps * ht)], whole[base_lt:used], cmid
        )
        gt_ref[:, h * ht : (h + 1) * ht, :] = taps_h.reshape(taps, ht, cmid)


def per_device(video, spatial_weight, spatial_bias, temporal_weight, temporal_bias, out_cotangent):
    W = lax.axis_size("wide")
    _, cin, R, cols = video.shape
    cmid = spatial_weight.shape[0]
    cout, taps, _ = temporal_weight.shape
    T = out_cotangent.shape[0]
    tr = out_cotangent.shape[2]
    F = W
    px = tr * cols
    half = taps // 2
    tscale = 1.0 / math.sqrt(T * R * cols)
    pscale = 1.0 / math.sqrt(F * R * cols)
    dma = pltpu.SemaphoreType.DMA
    vmem = pl.BlockSpec(memory_space=pltpu.VMEM)
    words = (cmid * 9 * cin + cout * taps * cmid) // 2
    rows = -(-words // (W * 128 * 16)) * 16

    v_rows = jnp.transpose(video[0], (1, 0, 2))
    g_rows = jnp.transpose(out_cotangent, (2, 0, 1, 3))
    ws = spatial_weight.reshape(cmid, 9 * cin)
    wt = temporal_weight.reshape(cout, taps * cmid)

    out, gv_rows, gs, gt = pl.pallas_call(
        functools.partial(block_kernel, W, tr, T, taps, rows, pscale, tscale),
        out_shape=(
            jax.ShapeDtypeStruct((T, cout, px), BF16),
            jax.ShapeDtypeStruct((R // 2, cin, cols), BF16),
            jax.ShapeDtypeStruct((cmid // 2, 9 * cin), F32),
            jax.ShapeDtypeStruct((taps, cout, cmid), F32),
        ),
        in_specs=[vmem] * 6,
        out_specs=(vmem,) * 4,
        scratch_shapes=[
            pltpu.VMEM((R + 4, cin, cols), BF16),
            pltpu.VMEM((F, tr + 4, cin, cols), BF16),
            pltpu.VMEM((2, T, cout, cols), BF16),
            pltpu.VMEM((tr + 4, 3, cin, cols), BF16),
            pltpu.VMEM(((T + half + 1) * cout, (tr + 2) * cols), BF16),
            pltpu.VMEM(((F + 2 * half) * cmid, px), BF16),
            pltpu.VMEM((cmid, 9 * cin), F32),
            pltpu.VMEM((F + 2 * (T - 1), cout, cmid), F32),
            pltpu.VMEM((3, 3 * cin, cmid), BF16),
            pltpu.VMEM((2, cmid, (half + 1) * cout), BF16),
            pltpu.VMEM((F, tr, cin, cols), BF16),
            pltpu.VMEM((cmid // 2, 9 * cin), F32),
            pltpu.VMEM((taps, cout // 2, cmid), F32),
            pltpu.VMEM((W * rows, 128), BF16),
            pltpu.VMEM((W, rows, 128), BF16),
            pltpu.VMEM((2, W * rows, 128), BF16),
        ]
        + [dma((W,))] * 4
        + [dma((2,))] * 4
        + [dma((W,))] * 8
        + [dma],
        compiler_params=pltpu.CompilerParams(
            collective_id=0, has_side_effects=True, vmem_limit_bytes=VMEM_BYTES
        ),
        name="space_time_block",
    )(v_rows, g_rows, ws, spatial_bias[:, None], wt, temporal_bias[:, None])

    grad_spatial = gs.reshape(cmid // 2, 9, cin)
    grad_temporal = jnp.transpose(gt, (1, 0, 2))
    grad_video = jnp.transpose(gv_rows, (1, 0, 2))[None]
    output = out.reshape(T, cout, tr, cols)
    return (output, grad_video, grad_spatial, grad_temporal)


def solution(mesh):
    in_specs = (
        P(("grp", "wide"), None, None, None),
        P(),
        P(),
        P(),
        P(),
        P("grp", None, ("wide", "narrow"), None),
    )
    out_specs = (
        P("grp", None, ("wide", "narrow"), None),
        P(("grp", "wide"), None, "narrow", None),
        P(("grp", "narrow"), None, None),
        P("grp", None, None),
    )
    return jax.shard_map(
        per_device, mesh=mesh, in_specs=in_specs, out_specs=out_specs, check_vma=False
    )
```

time: 65.7 us -> 49.8 us (0.76)
  Pallas kernels: 49.2 us -> 40.9 us
  local copies, waits for them, and re-layouts: 14.5 us -> 7.93 us
  other arithmetic: 0.92 us -> 0 us
    pallas_call x3 -> x1, Pallas kernels: 49.2 us -> 40.9 us  [per_device(): pl.pallas_call(functools.partial(block_kernel, W, tr, T, taps, rows, psca...]
    unnamed x22 -> x11, local copies, waits for them, and re-layouts: 8.67 us -> 4.47 us
    rev x1 -> x0, local copies, waits for them, and re-layouts: 1.62 us -> none  [per_device(): grid_w = spatial_weight.reshape(cmid, 3, 3, cin)[:, ::-1]]
    reshape x6 -> x0, local copies, waits for them, and re-layouts: 1.48 us -> none  [the longest x1 0.46 us: per_device(): gt.reshape(2, size_t)]
    pad x1 -> x0, local copies, waits for them, and re-layouts: 0.89 us -> none  [per_device(): jnp.pad(jnp.transpose(video[0], (1, 0, 2)), ((2, 2), (0, 0), (0, 0)))]
    pallas_call x0 -> x1, local copies, waits for them, and re-layouts: none -> 0.87 us  [per_device(): pl.pallas_call(functools.partial(block_kernel, W, tr, T, taps, rows, psca...]
    broadcast_in_dim x1, local copies, waits for them, and re-layouts: 0.1 us -> 0.79 us  [per_device(): temporal_bias[:, None]]
    broadcast_in_dim x1, local copies, waits for them, and re-layouts: 0.1 us -> 0.78 us  [per_device(): spatial_bias[:, None]]
where the time goes in v2:
time: 49.8 us; the launch traced here: 49.5 us
  Pallas kernels  40.9 us (82%)
  local copies, waits for them, and re-layouts  7.93 us (16%)
  between operations  0.68 us (1%)
    pallas_call x1, Pallas kernels, per_device(): pl.pallas_call(functools.partial(block_kernel, W, tr, T, taps, rows, psca...  40.9 us
    unnamed x11, local copies, waits for them, and re-layouts  4.47 us

profile of v2, /device:TPU:0, one launch (start us, length us, event | category | flops | bytes accessed | tf_op | source)
XLA Modules:
  0.0 49.5 jit_solution(14581059115591553562)
XLA Ops:
  0.6 0.0 copy-start.2
  0.6 0.8 %copy.23.tb_ref = f32[64,1]{1,0:T(8,128)S(1)} copy(f32[64,1]{0,1:T(1,128)} %bitcast.25) | data formatting | bytes 512 | tf_op jit(solution)/shard_map/broadcast_in_dim | solution.py:432
  1.4 0.8 %copy.21.sb_ref = f32[144,1]{1,0:T(8,128)S(1)} copy(f32[144,1]{0,1:T(1,128)} %bitcast.24) | data formatting | bytes 1152 | tf_op jit(solution)/shard_map/broadcast_in_dim | solution.py:432
  2.2 0.9 %copy.29 = bf16[4,64,2,128]{3,1,0,2:T(8,128)(2,1)S(1)} copy(bf16[4,64,2,128]{3,2,1,0:T(2,128)(2,1)} %param.11) | data formatting | bytes 262144 | tf_op args[5]
  3.1 0.0 copy-start.1
  3.2 0.0 copy-done.2
  3.2 0.2 copy.20.ws_ref
  3.3 0.8 %copy-done.1 = bf16[64,9,144]{2,0,1:T(8,128)(2,1)S(1)} copy-done((bf16[64,9,144]{2,0,1:T(8,128)(2,1)S(1)}, bf16[64,9,144]{2,0,1:T(8,128)(2,1)}, u32[]{:S(2)}) %copy-start.1) | copy-done | bytes 165912
  4.1 0.0 copy-start
  4.1 0.3 copy.19
  4.4 0.2 copy.22.wt_ref
  4.6 0.6 %copy-done = bf16[1,64,32,128]{3,2,1,0:T(8,128)(2,1)S(1)} copy-done((bf16[1,64,32,128]{3,2,1,0:T(8,128)(2,1)S(1)}, bf16[1,64,32,128]{3,2,1,0:T(8,128)(2,1)}, u32[]{:S(2)}) %copy-start) | copy-done | bytes 524312
  5.2 0.2 copy.28
  5.4 40.9 %space_time_block.1 = (bf16[4,64,256]{2,1,0:T(8,128)(2,1)S(1)}, bf16[16,64,128]{2,1,0:T(8,128)(2,1)S(1)}, f32[72,576]{1,0:T(8,128)S(1)}, f32[9,64,144]{2,1,0:T(8,128)S(1)}) custom-call(bf16[32,64,128]{2,1,0:T(8,128)(2,1)S(1)} %bitcast.17, bf16[2,4,64,128]{3,2,1,0:T(8,128)(2,1)S(1)} %bitcast.19, bf16[144,576]{1,0:T(8,128)(2,1)S(1)} %copy.20.ws_ref, ...), custom_call_target="tpu_custom_call" | custom-call | tf_op jit(solution)/shard_map/space_time_block/pallas_call | solution.py:396
  46.3 0.7 %reshape.22 = bf16[4,64,2,128]{3,2,1,0:T(2,128)(2,1)} reshape(bf16[4,64,256]{2,1,0:T(8,128)(2,1)S(1)} %get-tuple-element.8) | data formatting | bytes 262144 | tf_op jit(solution)/shard_map/reshape | solution.py:437
  47.0 0.9 %copy.25 = bf16[1,64,16,128]{3,2,1,0:T(8,128)(2,1)} copy(bf16[1,64,16,128]{3,1,2,0:T(8,128)(2,1)S(1)} %bitcast.20) | data formatting | bytes 524288
  47.9 0.9 %copy.24 = f32[72,576]{0,1:T(8,128)} copy(f32[72,576]{1,0:T(8,128)S(1)} %get-tuple-element.10) | data formatting | bytes 331776 | tf_op jit(solution)/shard_map/space_time_block/pallas_call | solution.py:396
  48.7 0.8 %copy.31 = f32[64,9,144]{2,0,1:T(8,128)} copy(f32[64,9,144]{2,0,1:T(8,128)S(1)} %bitcast.18) | data formatting | bytes 663552
Async XLA Ops:
  0.6 2.5 %copy-start.2 = (bf16[144,9,64]{0,2,1:T(8,128)(2,1)S(1)}, bf16[144,9,64]{0,2,1:T(8,128)(2,1)}, u32[]{:S(2)}) copy-start(bf16[144,9,64]{0,2,1:T(8,128)(2,1)} %param.7) | copy-start | bytes 497668
  3.1 1.0 %copy-start.1 = (bf16[64,9,144]{2,0,1:T(8,128)(2,1)S(1)}, bf16[64,9,144]{2,0,1:T(8,128)(2,1)}, u32[]{:S(2)}) copy-start(bf16[64,9,144]{2,0,1:T(8,128)(2,1)} %param.9) | copy-start | bytes 497668
  4.1 1.0 %copy-start = (bf16[1,64,32,128]{3,2,1,0:T(8,128)(2,1)S(1)}, bf16[1,64,32,128]{3,2,1,0:T(8,128)(2,1)}, u32[]{:S(2)}) copy-start(bf16[1,64,32,128]{3,2,1,0:T(8,128)(2,1)} %param.6) | copy-start | bytes 1572868

commit v3 on v2

--- a/solution.py
+++ b/solution.py
@@ -11,10 +11,11 @@
 MESH = pl.DeviceIdType.MESH
 BF16 = jnp.bfloat16
 F32 = jnp.float32
+LAG = 2
 VMEM_BYTES = 50 * 1024 * 1024
 
 
-def greet_all(wide_count):
+def greet_all(wide_count, between):
     me = lax.axis_index("wide") * 2 + lax.axis_index("narrow")
     total = 2 * wide_count
     barrier = pltpu.get_barrier_semaphore()
@@ -27,6 +28,7 @@
         return carry
 
     lax.fori_loop(1, total, greet, 0)
+    between()
     pl.semaphore_wait(barrier, total - 1)
 
 
@@ -72,9 +74,9 @@
     W, tr, T, taps, rows, pscale, tscale,
     v_ref, g_ref, ws_ref, sb_ref, wt_ref, tb_ref,
     out_ref, gvr_ref, gs_ref, gt_ref,
-    vpad, slab, halo, stack, gpad, apad, gsum, tsum, wv, wtap, gv,
+    slab, halo, stack, gpad, apad, gsum, tsum, wv, wtap, gv,
     nrs, nrt, sbuf, rbuf, full,
-    v_s, v_r, vf_s, vf_r, h_s, h_r, ns, nr, rs_s, rs_r, ag_s, ag_r, fw_s, fw_r, gv_s, gv_r, lsem,
+    v_s, v_r, vd_s, vd_r, vu_s, vu_r, h_s, h_r, ns, nr, rs_s, rs_r, ag_s, ag_r, fw_s, fw_r, gv_s, gv_r, lsem,
 ):
     F = W
     w = lax.axis_index("wide")
@@ -88,18 +90,17 @@
     gp_rows = tr + 2
     px = tr * cols
     rows6 = tr + 4
-    got = tr + 2
     even_taps = half + 1
     per = W // 2
     goal = w // per
     spot = lax.rem(w, per) * 2 + n
     low_tap = 2 * (T - 1) - half
-    place = 2 * n
-
-    vpad[0:2] = jnp.zeros((2, cin, cols), BF16)
-    vpad[R + 2 :] = jnp.zeros((2, cin, cols), BF16)
-    vpad[2 : R + 2] = v_ref[...]
-    greet_all(W)
+
+    def between():
+        for i in range(3):
+            wv[i] = ws_ref[:, 3 * cin * i : 3 * cin * (i + 1)].astype(F32).T.astype(BF16)
+
+    greet_all(W, between)
 
     nxt = lax.rem(me + 1, 2 * W)
     prv = lax.rem(me + 2 * W - 1, 2 * W)
@@ -110,24 +111,42 @@
 
     def v_copy(dst):
         return remote(
-            vpad.at[pl.ds(2 * tr * dst + got * n, got)], slab.at[w, pl.ds(place, got)], v_s.at[dst], v_r.at[w], dst, n
+            v_ref.at[pl.ds(2 * tr * dst + tr * n, tr)], slab.at[w, pl.ds(2, tr)], v_s.at[dst], v_r.at[w], dst, n
         )
 
     def v_arrival(src):
+        return remote(v_ref.at[pl.ds(0, tr)], slab.at[src, pl.ds(2, tr)], v_s.at[src], v_r.at[src], src, n)
+
+    def to_next(src):
         return remote(
-            vpad.at[pl.ds(0, got)], slab.at[src, pl.ds(place, got)], v_s.at[src], v_r.at[src], src, n
+            slab.at[src, pl.ds(tr, 2)], slab.at[src, pl.ds(0, 2)], vd_s.at[src], vd_r.at[src], nxt // 2, 1 - n
         )
 
-    def v_forward(src):
+    def to_prev(src):
         return remote(
-            slab.at[src, pl.ds(tr * (1 - n) + 2 * n, 2)], slab.at[src, pl.ds(got * n, 2)],
-            vf_s.at[src], vf_r.at[src], w, 1 - n,
+            slab.at[src, pl.ds(2, 2)], slab.at[src, pl.ds(tr + 2, 2)], vu_s.at[src], vu_r.at[src], prv // 2, 1 - n
         )
 
-    def v_forwarded(src):
-        return remote(
-            slab.at[src, pl.ds(0, 2)], slab.at[src, pl.ds(got * (1 - n), 2)], vf_s.at[src], vf_r.at[src], w, 1 - n
-        )
+    sends_down = me < 2 * W - 1
+    sends_up = me > 0
+
+    def hand_on(src, act):
+        @pl.when(jnp.logical_and(sends_down, src != nxt // 2))
+        def _():
+            act(to_next(src))
+
+        @pl.when(jnp.logical_and(sends_up, src != prv // 2))
+        def _():
+            act(to_prev(src))
+
+    def await_halo(src):
+        @pl.when(sends_up)
+        def _():
+            to_next(src).wait_recv()
+
+        @pl.when(sends_down)
+        def _():
+            to_prev(src).wait_recv()
 
     def gv_copy(f):
         return remote(gv.at[f], gvr_ref.at[pl.ds(spot * tr, tr)], gv_s.at[f], gv_r.at[spot], f, goal)
@@ -140,9 +159,28 @@
 
     lax.fori_loop(1, W, start, 0)
 
-    slab[w] = vpad[pl.ds(2 * tr * w + tr * n, rows6)]
-    for i in range(3):
-        wv[i] = ws_ref[:, 3 * cin * i : 3 * cin * (i + 1)].astype(F32).T.astype(BF16)
+    slab[w, 2 : 2 + tr] = v_ref[pl.ds(tr * me, tr)]
+    hand_on(w, lambda copy: copy.start())
+    edge = jnp.zeros((2, cin, cols), BF16)
+
+    @pl.when(sends_up)
+    def _():
+        slab[w, 0:2] = v_ref[pl.ds(jnp.maximum(tr * me - 2, 0), 2)]
+
+    @pl.when(sends_down)
+    def _():
+        slab[w, tr + 2 :] = v_ref[pl.ds(jnp.minimum(tr * me + tr, R - 2), 2)]
+
+    @pl.when(jnp.logical_not(sends_up))
+    def _():
+        for f in range(F):
+            slab[f, 0:2] = edge
+
+    @pl.when(jnp.logical_not(sends_down))
+    def _():
+        for f in range(F):
+            slab[f, tr + 2 :] = edge
+
     for parity in range(2):
         for m in range(even_taps):
             k = taps - 1 - parity - 2 * m
@@ -168,6 +206,8 @@
     below = halo[1].reshape(T * cout, cols)
     gpad[body, (tr + 1) * cols :] = jnp.where(me == 2 * W - 1, jnp.zeros_like(below), below)
 
+    sb = jnp.broadcast_to(sb_ref[...], (8, cmid)).T[:, 0:1]
+    tb = jnp.broadcast_to(tb_ref[...], (8, cout)).T[:, 0:1]
     lane = lax.broadcasted_iota(jnp.int32, (rows6 * cin, cols), 1)
     lane_out = lax.broadcasted_iota(jnp.int32, (cin, cols), 1)
 
@@ -182,7 +222,7 @@
         big = jnp.concatenate(
             [stack[r : r + 3].reshape(9 * cin, cols) for r in range(gp_rows)], axis=1
         )
-        pre = jnp.dot(ws_ref[...], big, preferred_element_type=F32) + sb_ref[...]
+        pre = jnp.dot(ws_ref[...], big, preferred_element_type=F32) + sb
         s = 1.0 / (1.0 + jnp.exp(-pre))
         act = (pre[:, cols : cols + px] * s[:, cols : cols + px]).astype(BF16)
         apad[pl.ds(pl.multiple_of((f + half) * cmid, 16), cmid), :] = act
@@ -216,19 +256,22 @@
     def _():
         gv_copy(w).start()
 
-    v_arrival(lax.rem(w + W - 1, W)).wait_recv()
-    v_forward(lax.rem(w + W - 1, W)).start()
+    def take(k):
+        src = lax.rem(w + 2 * W - k, W)
+        v_arrival(src).wait_recv()
+        hand_on(src, lambda copy: copy.start())
+
+    for k in range(1, 1 + LAG):
+        take(k)
 
     def each(k, carry):
         src = lax.rem(w + W - k, W)
-        after = lax.rem(w + W - k - 1, W)
-
-        @pl.when(k < W - 1)
+
+        @pl.when(k < W - LAG)
         def _():
-            v_arrival(after).wait_recv()
-            v_forward(after).start()
-
-        v_forwarded(src).wait_recv()
+            take(k + LAG)
+
+        await_halo(src)
         frame(src)
         gv_copy(src).start()
         return carry
@@ -273,7 +316,7 @@
 
     def step(t, carry):
         a = apad[pl.ds(pl.multiple_of(2 * t * cmid, 16), taps * cmid), :]
-        o = jnp.dot(wt_ref[...], a, preferred_element_type=F32) + tb_ref[...]
+        o = jnp.dot(wt_ref[...], a, preferred_element_type=F32) + tb
         out_ref[t] = o.astype(BF16)
         return carry
 
@@ -323,13 +366,15 @@
     def finish(k, carry):
         other = lax.rem(w + k, W)
         v_copy(other).wait_send()
-        v_forward(other).wait_send()
+        hand_on(other, lambda copy: copy.wait_send())
         rs_copy(other).wait_send()
         ag_copy(other).wait_send()
         gv_copy(other).wait_send()
         return carry
 
     lax.fori_loop(1, W, finish, 0)
+
+    hand_on(w, lambda copy: copy.wait_send())
 
     def finish_fw(s, carry):
         remote(
@@ -404,7 +449,6 @@
         in_specs=[vmem] * 6,
         out_specs=(vmem,) * 4,
         scratch_shapes=[
-            pltpu.VMEM((R + 4, cin, cols), BF16),
             pltpu.VMEM((F, tr + 4, cin, cols), BF16),
             pltpu.VMEM((2, T, cout, cols), BF16),
             pltpu.VMEM((tr + 4, 3, cin, cols), BF16),
@@ -421,7 +465,7 @@
             pltpu.VMEM((W, rows, 128), BF16),
             pltpu.VMEM((2, W * rows, 128), BF16),
         ]
-        + [dma((W,))] * 4
+        + [dma((W,))] * 6
         + [dma((2,))] * 4
         + [dma((W,))] * 8
         + [dma],
@@ -429,7 +473,7 @@
             collective_id=0, has_side_effects=True, vmem_limit_bytes=VMEM_BYTES
         ),
         name="space_time_block",
-    )(v_rows, g_rows, ws, spatial_bias[:, None], wt, temporal_bias[:, None])
+    )(v_rows, g_rows, ws, spatial_bias[None], wt, temporal_bias[None])
 
     grad_spatial = gs.reshape(cmid // 2, 9, cin)
     grad_temporal = jnp.transpose(gt, (1, 0, 2))

time: 49.8 us -> 47.5 us (0.954)
  Pallas kernels: 40.9 us -> 39.4 us
  local copies, waits for them, and re-layouts: 7.93 us -> 7.25 us
    pallas_call x1, Pallas kernels: 40.9 us -> 39.4 us  [per_device(): pl.pallas_call(functools.partial(block_kernel, W, tr, T, taps, rows, psca...]
    broadcast_in_dim x2 -> x0, local copies, waits for them, and re-layouts: 1.56 us -> none  [the longest x1 0.79 us: per_device(): temporal_bias[:, None]]
    reshape x1, local copies, waits for them, and re-layouts: 0.16 us -> 1.17 us  [per_device(): ws = spatial_weight.reshape(cmid, 9 * cin)]
    unnamed x11 -> x13, local copies, waits for them, and re-layouts: 4.47 us -> 4.34 us
where the time goes in v3:
time: 47.5 us; the launch traced here: 47.3 us
  Pallas kernels  39.4 us (83%)
  local copies, waits for them, and re-layouts  7.25 us (15%)
  between operations  0.69 us (1%)
    pallas_call x1, Pallas kernels, per_device(): pl.pallas_call(functools.partial(block_kernel, W, tr, T, taps, rows, psca...  39.4 us
    unnamed x13, local copies, waits for them, and re-layouts  4.34 us
    reshape x1, local copies, waits for them, and re-layouts, per_device(): ws = spatial_weight.reshape(cmid, 9 * cin)  1.17 us

profile of v3, /device:TPU:0, one launch (start us, length us, event | category | flops | bytes accessed | tf_op | source)
XLA Modules:
  0.0 47.3 jit_solution(14066501990233117167)
XLA Ops:
  0.6 0.9 %copy.26 = bf16[4,64,2,128]{3,1,0,2:T(8,128)(2,1)S(1)} copy(bf16[4,64,2,128]{3,2,1,0:T(2,128)(2,1)} %param.11) | data formatting | bytes 262144 | tf_op args[5]
  1.6 0.0 copy-start.3
  1.6 1.2 %copy.19.ws_ref = bf16[144,576]{1,0:T(8,128)(2,1)S(1)} copy(bf16[144,576]{0,1:T(8,128)(2,1)} %bitcast.24) | data formatting | bytes 331776 | tf_op jit(solution)/shard_map/reshape | solution.py:438
  2.7 0.0 copy-done.3
  2.7 0.0 copy-start.2
  2.8 0.3 copy.18
  3.0 0.2 copy.20.wt_ref
  3.2 0.6 %copy-done.2 = bf16[1,64,32,128]{3,2,1,0:T(8,128)(2,1)S(1)} copy-done((bf16[1,64,32,128]{3,2,1,0:T(8,128)(2,1)S(1)}, bf16[1,64,32,128]{3,2,1,0:T(8,128)(2,1)}, u32[]{:S(2)}) %copy-start.2) | copy-done | bytes 524312
  3.8 0.2 copy.25
  4.0 0.0 copy-start
  4.0 0.0 copy-start.1
  4.0 0.7 %copy-done = f32[144]{0:T(256)S(1)} copy-done((f32[144]{0:T(256)S(1)}, f32[144]{0:T(256)}, u32[]{:S(2)}) %copy-start) | copy-done | bytes 600
  4.7 0.0 copy-done.1
  4.7 39.4 %space_time_block.1 = (bf16[4,64,256]{2,1,0:T(8,128)(2,1)S(1)}, bf16[16,64,128]{2,1,0:T(8,128)(2,1)S(1)}, f32[72,576]{1,0:T(8,128)S(1)}, f32[9,64,144]{2,1,0:T(8,128)S(1)}) custom-call(bf16[32,64,128]{2,1,0:T(8,128)(2,1)S(1)} %bitcast.17, bf16[2,4,64,128]{3,2,1,0:T(8,128)(2,1)S(1)} %bitcast.19, bf16[144,576]{1,0:T(8,128)(2,1)S(1)} %copy.19.ws_ref, ...), custom_call_target="tpu_custom_call" | custom-call | tf_op jit(solution)/shard_map/space_time_block/pallas_call | solution.py:441
  44.1 0.7 %reshape.22 = bf16[4,64,2,128]{3,2,1,0:T(2,128)(2,1)} reshape(bf16[4,64,256]{2,1,0:T(8,128)(2,1)S(1)} %get-tuple-element.8) | data formatting | bytes 262144 | tf_op jit(solution)/shard_map/reshape | solution.py:481
  44.7 0.9 %copy.22 = bf16[1,64,16,128]{3,2,1,0:T(8,128)(2,1)} copy(bf16[1,64,16,128]{3,1,2,0:T(8,128)(2,1)S(1)} %bitcast.20) | data formatting | bytes 524288
  45.6 0.9 %copy.21 = f32[72,576]{0,1:T(8,128)} copy(f32[72,576]{1,0:T(8,128)S(1)} %get-tuple-element.10) | data formatting | bytes 331776 | tf_op jit(solution)/shard_map/space_time_block/pallas_call | solution.py:441
  46.5 0.8 %copy.28 = f32[64,9,144]{2,0,1:T(8,128)} copy(f32[64,9,144]{2,0,1:T(8,128)S(1)} %bitcast.18) | data formatting | bytes 663552
Async XLA Ops:
  1.6 1.2 %copy-start.3 = (bf16[64,9,144]{2,0,1:T(8,128)(2,1)S(1)}, bf16[64,9,144]{2,0,1:T(8,128)(2,1)}, u32[]{:S(2)}) copy-start(bf16[64,9,144]{2,0,1:T(8,128)(2,1)} %param.9) | copy-start | bytes 497668
  2.7 1.0 %copy-start.2 = (bf16[1,64,32,128]{3,2,1,0:T(8,128)(2,1)S(1)}, bf16[1,64,32,128]{3,2,1,0:T(8,128)(2,1)}, u32[]{:S(2)}) copy-start(bf16[1,64,32,128]{3,2,1,0:T(8,128)(2,1)} %param.6) | copy-start | bytes 1572868
  4.0 0.7 %copy-start = (f32[144]{0:T(256)S(1)}, f32[144]{0:T(256)}, u32[]{:S(2)}) copy-start(f32[144]{0:T(256)} %param.8) | copy-start | bytes 1732
  4.0 0.7 %copy-start.1 = (f32[64]{0:T(128)S(1)}, f32[64]{0:T(128)}, u32[]{:S(2)}) copy-start(f32[64]{0:T(128)} %param.10) | copy-start | bytes 772

commit v4 on v3

--- a/solution.py
+++ b/solution.py
@@ -11,7 +11,6 @@
 MESH = pl.DeviceIdType.MESH
 BF16 = jnp.bfloat16
 F32 = jnp.float32
-LAG = 2
 VMEM_BYTES = 50 * 1024 * 1024
 
 
@@ -261,15 +260,11 @@
         v_arrival(src).wait_recv()
         hand_on(src, lambda copy: copy.start())
 
-    for k in range(1, 1 + LAG):
+    for k in range(1, W):
         take(k)
 
     def each(k, carry):
         src = lax.rem(w + W - k, W)
-
-        @pl.when(k < W - LAG)
-        def _():
-            take(k + LAG)
 
         await_halo(src)
         frame(src)

time: 47.5 us -> 43.8 us (0.922)
  Pallas kernels: 39.4 us -> 35.6 us
    pallas_call x1, Pallas kernels: 39.4 us -> 35.6 us  [per_device(): pl.pallas_call(functools.partial(block_kernel, W, tr, T, taps, rows, psca...]
where the time goes in v4:
time: 43.8 us; the launch traced here: 43.6 us
  Pallas kernels  35.6 us (81%)
  local copies, waits for them, and re-layouts  7.25 us (17%)
  between operations  0.69 us (2%)
    pallas_call x1, Pallas kernels, per_device(): pl.pallas_call(functools.partial(block_kernel, W, tr, T, taps, rows, psca...  35.6 us
    unnamed x13, local copies, waits for them, and re-layouts  4.34 us
    reshape x1, local copies, waits for them, and re-layouts, per_device(): ws = spatial_weight.reshape(cmid, 9 * cin)  1.17 us

profile of v4, /device:TPU:0, one launch (start us, length us, event | category | flops | bytes accessed | tf_op | source)
XLA Modules:
  0.0 43.6 jit_solution(1012549135620078235)
XLA Ops:
  0.6 0.9 %copy.26 = bf16[4,64,2,128]{3,1,0,2:T(8,128)(2,1)S(1)} copy(bf16[4,64,2,128]{3,2,1,0:T(2,128)(2,1)} %param.11) | data formatting | bytes 262144 | tf_op args[5]
  1.6 0.0 copy-start.3
  1.6 1.2 %copy.19.ws_ref = bf16[144,576]{1,0:T(8,128)(2,1)S(1)} copy(bf16[144,576]{0,1:T(8,128)(2,1)} %bitcast.24) | data formatting | bytes 331776 | tf_op jit(solution)/shard_map/reshape | solution.py:433
  2.7 0.0 copy-done.3
  2.7 0.0 copy-start.2
  2.8 0.3 copy.18
  3.0 0.2 copy.20.wt_ref
  3.2 0.6 %copy-done.2 = bf16[1,64,32,128]{3,2,1,0:T(8,128)(2,1)S(1)} copy-done((bf16[1,64,32,128]{3,2,1,0:T(8,128)(2,1)S(1)}, bf16[1,64,32,128]{3,2,1,0:T(8,128)(2,1)}, u32[]{:S(2)}) %copy-start.2) | copy-done | bytes 524312
  3.8 0.2 copy.25
  4.0 0.0 copy-start
  4.0 0.0 copy-start.1
  4.0 0.7 %copy-done = f32[144]{0:T(256)S(1)} copy-done((f32[144]{0:T(256)S(1)}, f32[144]{0:T(256)}, u32[]{:S(2)}) %copy-start) | copy-done | bytes 600
  4.7 0.0 copy-done.1
  4.7 35.6 %space_time_block.1 = (bf16[4,64,256]{2,1,0:T(8,128)(2,1)S(1)}, bf16[16,64,128]{2,1,0:T(8,128)(2,1)S(1)}, f32[72,576]{1,0:T(8,128)S(1)}, f32[9,64,144]{2,1,0:T(8,128)S(1)}) custom-call(bf16[32,64,128]{2,1,0:T(8,128)(2,1)S(1)} %bitcast.17, bf16[2,4,64,128]{3,2,1,0:T(8,128)(2,1)S(1)} %bitcast.19, bf16[144,576]{1,0:T(8,128)(2,1)S(1)} %copy.19.ws_ref, ...), custom_call_target="tpu_custom_call" | custom-call | tf_op jit(solution)/shard_map/space_time_block/pallas_call | solution.py:436
  40.3 0.7 %reshape.22 = bf16[4,64,2,128]{3,2,1,0:T(2,128)(2,1)} reshape(bf16[4,64,256]{2,1,0:T(8,128)(2,1)S(1)} %get-tuple-element.8) | data formatting | bytes 262144 | tf_op jit(solution)/shard_map/reshape | solution.py:476
  41.0 0.9 %copy.22 = bf16[1,64,16,128]{3,2,1,0:T(8,128)(2,1)} copy(bf16[1,64,16,128]{3,1,2,0:T(8,128)(2,1)S(1)} %bitcast.20) | data formatting | bytes 524288
  41.9 0.9 %copy.21 = f32[72,576]{0,1:T(8,128)} copy(f32[72,576]{1,0:T(8,128)S(1)} %get-tuple-element.10) | data formatting | bytes 331776 | tf_op jit(solution)/shard_map/space_time_block/pallas_call | solution.py:436
  42.8 0.8 %copy.28 = f32[64,9,144]{2,0,1:T(8,128)} copy(f32[64,9,144]{2,0,1:T(8,128)S(1)} %bitcast.18) | data formatting | bytes 663552
Async XLA Ops:
  1.6 1.2 %copy-start.3 = (bf16[64,9,144]{2,0,1:T(8,128)(2,1)S(1)}, bf16[64,9,144]{2,0,1:T(8,128)(2,1)}, u32[]{:S(2)}) copy-start(bf16[64,9,144]{2,0,1:T(8,128)(2,1)} %param.9) | copy-start | bytes 497668
  2.7 1.0 %copy-start.2 = (bf16[1,64,32,128]{3,2,1,0:T(8,128)(2,1)S(1)}, bf16[1,64,32,128]{3,2,1,0:T(8,128)(2,1)}, u32[]{:S(2)}) copy-start(bf16[1,64,32,128]{3,2,1,0:T(8,128)(2,1)} %param.6) | copy-start | bytes 1572868
  4.0 0.7 %copy-start = (f32[144]{0:T(256)S(1)}, f32[144]{0:T(256)}, u32[]{:S(2)}) copy-start(f32[144]{0:T(256)} %param.8) | copy-start | bytes 1732
  4.0 0.7 %copy-start.1 = (f32[64]{0:T(128)S(1)}, f32[64]{0:T(128)}, u32[]{:S(2)}) copy-start(f32[64]{0:T(128)} %param.10) | copy-start | bytes 772
